TPU v7x, 128 devices: a whole 4x4x4 slice. The times are simulated.
128 devices in a mesh: blk: 8 (over y_lo, x), vslab: 16 (over z, y_hi, core).
Axes of the slice: x: 4, y: 4 (y_hi: 2, y_lo: 2; y = y_hi * 2 + y_lo), z: 4, core: 2. Of those that a mesh axis runs over, the one named last changes fastest.
Arguments:
- amplitudes: float32 [1024, 128, 800], P('blk', 'vslab'), may hold values from -6 to 6
- integrals: float32 [128, 800, 4096], P('vslab', None, 'blk'), may hold values from -0.01953125 to 0.01953125
- ab_energy: float32 [4096], P('blk'), may hold values from 1 to 4
- ij_energy: float32 [1024], replicated, may hold values from -4 to -1
- block_size: int32 [32], replicated, may hold values from 1 to 95, as said below
- block_owner: int32 [32], replicated, may hold values from 0 to 15, as said below
Outputs:
- amplitude_new: float32 [1024, 12288], P(None, ('blk', 'vslab'))
Inputs may be any that keep to these rules, and one draw needn't show every extreme that they name: `block_size`: the blocks of one group fill its 512 pairs exactly; every owner holds at most 96 pairs, and one owner exactly 96. `block_owner`: every owner has two blocks.
All inputs are finite; a program needn't handle non-finite values.
Results may differ from a plain program's by a relative error of at most 0.00007.
Values sent between devices are 32-bit elements; how exact they have to be, the bound alone decides.
No kernel may reach another device: no remote copies, remote signals or barrier semaphores. Data moves between devices by JAX's collectives and lax.ppermute only.
A program may use at most 128 MiB of HBM per device.

v0:
```python
import jax
import jax.numpy as jnp
from jax import lax
from jax.sharding import PartitionSpec as P


def slot_tables(block_size, block_owner, rows, owners, cap):
    count = block_size.shape[0]
    order = jnp.arange(count, dtype=jnp.int32)
    starts = jnp.cumsum(block_size) - block_size
    same = block_owner[:, None] == block_owner[None, :]
    earlier = order[None, :] < order[:, None]
    before = jnp.sum(jnp.where(same & earlier, block_size[None, :], 0), axis=1)
    owner_hot = block_owner[:, None] == jnp.arange(owners, dtype=jnp.int32)[None, :]
    load = jnp.sum(jnp.where(owner_hot, block_size[:, None], 0), axis=0)
    owner_start = jnp.cumsum(load) - load
    block_base = jnp.sum(jnp.where(owner_hot, owner_start[None, :], 0), axis=1)
    shift_by = block_base + before - starts
    row_ids = jnp.arange(rows, dtype=jnp.int32)
    inside = (row_ids[:, None] >= starts[None, :]) & (
        row_ids[:, None] < (starts + block_size)[None, :]
    )
    position = jnp.sum(jnp.where(inside, shift_by[None, :], 0), axis=1) + row_ids
    perm = jnp.zeros((rows,), jnp.int32).at[position].set(row_ids)
    slot_ids = jnp.arange(cap, dtype=jnp.int32)
    valid = slot_ids[None, :] < load[:, None]
    index = jnp.minimum(owner_start[:, None] + slot_ids[None, :], rows - 1)
    source = perm[index]
    return (perm, owner_start, load, source, valid)


def on_device(amplitudes, integrals, ab_energy, ij_energy, block_size, block_owner):
    owners = lax.axis_size("vslab")
    rows = integrals.shape[2]
    cap = 3 * rows // owners
    v_matrix = integrals.reshape(-1, rows)
    t_tile = amplitudes.reshape(amplitudes.shape[0], -1)
    ladder = jnp.dot(
        lax.all_gather(t_tile, "blk", axis=0, tiled=True),
        v_matrix,
        precision=lax.Precision.HIGHEST,
        preferred_element_type=jnp.float32,
    )
    perm, owner_start, load, source, valid = slot_tables(block_size, block_owner, rows, owners, cap)
    mine = lax.axis_index("vslab")
    my_source = lax.dynamic_index_in_dim(source, mine, 0, keepdims=False)
    my_valid = lax.dynamic_index_in_dim(valid, mine, 0, keepdims=False)
    packed = jnp.take(ladder, source.reshape(-1), axis=1)
    packed = jnp.where(valid.reshape(1, -1), packed, 0.0).reshape(ladder.shape[0], owners, cap)
    received = lax.all_to_all(packed, "vslab", split_axis=1, concat_axis=1, tiled=True)
    summed = jnp.sum(received, axis=1)
    denom = jnp.take(ab_energy, my_source)[None, :] - ij_energy[:, None]
    return jnp.where(my_valid[None, :], summed / denom, 0.0)


def solution(mesh):
    placed = (P("blk", "vslab", None), P("vslab", None, "blk"), P("blk"), P(), P(), P())
    return jax.shard_map(
        on_device, mesh=mesh, in_specs=placed, out_specs=P(None, ("blk", "vslab")), check_vma=False
    )
```

profile of v0, /device:TPU:1, one launch (start us, length us, event | category | flops | bytes accessed | tf_op | source)
XLA Modules:
  0.0 425.9 jit_solution(8877421864067574619)
XLA Ops:
  6.5 0.0 copy-start
  6.5 0.0 all-gather.2.cloned.1.call-start
  6.5 0.7 all-gather.2.cloned.1.call-update
  7.3 0.8 select_reduce_fusion.3
  8.0 0.1 copy.14
  8.2 0.1 reduce.1
  8.3 0.7 copy.13
  9.0 0.1 reduce-window.15
  9.1 0.1 reduce
  9.2 0.1 compare_select_fusion.2
  9.3 0.1 reshape.231
  9.4 0.7 select_reduce_fusion.2
  10.1 0.9 select_reduce_fusion.1
  11.0 0.7 add_subtract_fusion
  11.7 0.1 select_reduce_fusion
  11.8 2.4 scatter_custom_fusion
  14.3 9.5 %gather_fusion = s32[1536]{0:T(1024)S(1)} fusion(s32[512]{0:T(512)S(1)} %scatter_custom_fusion, s32[2048]{0:T(1024)S(1)} %pad_clamp_fusion.1), kind=kCustom, calls=%fused_computation | custom fusion | bytes 18432 | tf_op jit(solution)/shard_map/gather | solution.py:28
  23.7 0.1 reshape.230
  23.8 0.1 iota_compare_fusion.4
  23.9 250.5 %all-gather.2.cloned.1.call-done = f32[1024,6400]{0,1:T(8,128)} async-done(((f32[128,6400]{0,1:T(8,128)}), f32[1024,6400]{0,1:T(8,128)}) %all-gather.2.cloned.1.call-update) | async-done | bytes 26214416 | tf_op jit(solution)/shard_map/all_gather | solution.py:39
  274.4 45.6 %fusion.7 = f32[1024,512]{0,1:T(8,128)S(1)} fusion(f32[1024,6400]{0,1:T(8,128)} %all-gather.2.cloned.1.call-done, f32[6400,512]{1,0:T(8,128)} %bitcast.31), kind=kOutput, calls=%fused_computation.36 | convolution fusion | flops 40265318400 | bytes 41418752 | tf_op jit(solution)/shard_map/dot_general | solution.py:38
  320.0 5.8 %gather_fusion.1 = f32[1536,1024]{1,0:T(8,128)} fusion(f32[1024,512]{0,1:T(8,128)S(1)} %fusion.7, s32[2048]{0:T(1024)S(1)} %pad_clamp_fusion), kind=kCustom, calls=%fused_computation.1 | custom fusion | bytes 12589056 | tf_op jit(solution)/shard_map/jit(_take)/gather | solution.py:48
  325.8 4.9 %select_select_fusion = f32[1024,16,96]{0,2,1:T(8,128)} fusion(f32[1024,16,96]{0,2,1:T(8,128)} %bitcast.25, pred[16,96]{1,0:T(8,128)(4,1)S(1)} %get-tuple-element.8, pred[16,96]{1,0:T(8,128)(4,1)S(1)} %get-tuple-element.7), kind=kLoop, calls=%fused_computation.4 | loop fusion | flops 3145728 | bytes 12585984 | tf_op jit(solution)/shard_map/jit(_where)/select_n | solution.py:49
  330.8 10.5 %all-to-all-start = ((f32[1024,16,96]{0,2,1:T(8,128)}), f32[1024,16,96]{0,2,1:T(8,128)}, u32[]{:S(2)}, u32[]{:S(2)}) async-start(f32[1024,16,96]{0,2,1:T(8,128)} %select_select_fusion), calls=%async_computation | async-start | bytes 12582912 | tf_op jit(solution)/shard_map/all_to_all | solution.py:50
  341.2 0.0 copy-start.1
  341.3 0.0 copy-done
  341.3 1.3 gather_fusion.2
  342.6 72.2 %all-to-all-done = f32[1024,16,96]{0,2,1:T(8,128)} async-done(((f32[1024,16,96]{0,2,1:T(8,128)}), f32[1024,16,96]{0,2,1:T(8,128)}, u32[]{:S(2)}, u32[]{:S(2)}) %all-to-all-start) | async-done | bytes 6291488 | tf_op jit(solution)/shard_map/all_to_all | solution.py:50
  414.8 3.4 reduce_sum.52
  418.2 0.0 copy-done.1
  418.2 0.9 divide_select_fusion
  (11 shorter events, 0.1 us)
Async XLA Ops:
  6.5 334.7 %copy-start = (f32[512]{0:T(512)S(1)}, f32[512]{0:T(512)}, u32[]{:S(2)}) copy-start(f32[512]{0:T(512)} %param.8) | copy-start | bytes 6148
  6.5 267.8 %all-gather.2.cloned.1.call-start = ((), (), s32[]{:S(2)}) async-start(), calls=%async_computation.1 | async-start | bytes 29491200 | tf_op jit(solution)/shard_map/all_gather | solution.py:39
  330.8 84.0 %all-to-all-start = ((f32[1024,16,96]{0,2,1:T(8,128)}), f32[1024,16,96]{0,2,1:T(8,128)}, u32[]{:S(2)}, u32[]{:S(2)}) async-start(f32[1024,16,96]{0,2,1:T(8,128)} %select_select_fusion), calls=%async_computation | async-start | bytes 12582912 | tf_op jit(solution)/shard_map/all_to_all | solution.py:50
  341.2 76.9 %copy-start.1 = (f32[1024]{0:T(1024)S(1)}, f32[1024]{0:T(1024)}, u32[]{:S(2)}) copy-start(f32[1024]{0:T(1024)} %param.9) | copy-start | bytes 12292
Sparse Core Ops, SparseCore 0:
  8.9 265.4 all-gather.1
where the time goes:
time: 426 us
  waiting for transfers between devices  323 us (76%)
  matrix products  45.6 us (11%)
  local copies, waits for them, and re-layouts  20 us (5%)
  between operations  13.5 us (3%)
  other arithmetic  13 us (3%)
  starting transfers between devices  10.5 us (2%)
    all_gather x1, waiting for transfers between devices, on_device(): lax.all_gather(t_tile, 'blk', axis=0, tiled=True)  250 us
    all_to_all x1, waiting for transfers between devices, on_device(): lax.all_to_all(packed, 'vslab', split_axis=1, concat_axis=1, tiled=True)  72.2 us
    dot_general x1, matrix products, on_device(): jnp.dot(lax.all_gather(t_tile, 'blk', axis=0, tiled=True), v_matrix, prec...  45.6 us
    all_to_all x1, starting transfers between devices, on_device(): lax.all_to_all(packed, 'vslab', split_axis=1, concat_axis=1, tiled=True)  10.5 us
    gather x2, local copies, waits for them, and re-layouts, slot_tables(): source = perm[index]  9.54 us
  transfers between devices with their start and end apart: 2, of which 2 were waited for; matrix products, arithmetic and copies ran while one was open for 4% of the time, Pallas kernels for 0%

commit v1 on v0

--- a/solution.py
+++ b/solution.py
@@ -7,13 +7,15 @@
 def slot_tables(block_size, block_owner, rows, owners, cap):
     count = block_size.shape[0]
     order = jnp.arange(count, dtype=jnp.int32)
-    starts = jnp.cumsum(block_size) - block_size
+    before_me = order[None, :] < order[:, None]
+    starts = jnp.sum(jnp.where(before_me, block_size[None, :], 0), axis=1)
     same = block_owner[:, None] == block_owner[None, :]
-    earlier = order[None, :] < order[:, None]
+    earlier = before_me
     before = jnp.sum(jnp.where(same & earlier, block_size[None, :], 0), axis=1)
     owner_hot = block_owner[:, None] == jnp.arange(owners, dtype=jnp.int32)[None, :]
     load = jnp.sum(jnp.where(owner_hot, block_size[:, None], 0), axis=0)
-    owner_start = jnp.cumsum(load) - load
+    owner_ids = jnp.arange(owners, dtype=jnp.int32)
+    owner_start = jnp.sum(jnp.where(owner_ids[None, :] < owner_ids[:, None], load[None, :], 0), axis=1)
     block_base = jnp.sum(jnp.where(owner_hot, owner_start[None, :], 0), axis=1)
     shift_by = block_base + before - starts
     row_ids = jnp.arange(rows, dtype=jnp.int32)

time: 426 us -> 426 us (level)
  no operation moved by 1% of the time
where the time goes in v1:
time: 426 us
  waiting for transfers between devices  324 us (76%)
  matrix products  45.6 us (11%)
  local copies, waits for them, and re-layouts  19.2 us (5%)
  between operations  13.5 us (3%)
  other arithmetic  12.7 us (3%)
  starting transfers between devices  10.4 us (2%)
    all_gather x1, waiting for transfers between devices, on_device(): lax.all_gather(t_tile, 'blk', axis=0, tiled=True)  252 us
    all_to_all x1, waiting for transfers between devices, on_device(): lax.all_to_all(packed, 'vslab', split_axis=1, concat_axis=1, tiled=True)  72.2 us
    dot_general x1, matrix products, on_device(): jnp.dot(lax.all_gather(t_tile, 'blk', axis=0, tiled=True), v_matrix, prec...  45.6 us
    all_to_all x1, starting transfers between devices, on_device(): lax.all_to_all(packed, 'vslab', split_axis=1, concat_axis=1, tiled=True)  10.4 us
    gather x2, local copies, waits for them, and re-layouts, slot_tables(): source = perm[index]  9.54 us
  transfers between devices with their start and end apart: 2, of which 2 were waited for; matrix products, arithmetic and copies ran while one was open for 4% of the time, Pallas kernels for 0%

profile of v1, /device:TPU:1, one launch (start us, length us, event | category | flops | bytes accessed | tf_op | source)
XLA Modules:
  0.0 425.9 jit_solution(9916567833174694342)
XLA Ops:
  6.5 0.0 copy-start
  6.5 0.0 all-gather.2.cloned.1.call-start
  6.5 0.7 all-gather.2.cloned.1.call-update
  7.3 0.8 select_reduce_fusion.5
  8.0 0.1 select_reduce_fusion.4
  8.2 0.1 compare_select_fusion.2
  8.2 0.1 reshape.187
  8.3 0.8 select_reduce_fusion.3
  9.1 0.9 select_reduce_fusion.1
  10.0 0.7 fusion.7
  10.6 0.1 select_reduce_fusion
  10.8 2.4 scatter_custom_fusion
  13.2 9.5 %gather_fusion = s32[1536]{0:T(1024)S(1)} fusion(s32[512]{0:T(512)S(1)} %scatter_custom_fusion, s32[2048]{0:T(1024)S(1)} %pad_clamp_fusion.1), kind=kCustom, calls=%fused_computation | custom fusion | bytes 18432 | tf_op jit(solution)/shard_map/gather | solution.py:30
  22.7 0.1 reshape.186
  22.8 0.1 iota_compare_fusion.5
  22.9 251.6 %all-gather.2.cloned.1.call-done = f32[1024,6400]{0,1:T(8,128)} async-done(((f32[128,6400]{0,1:T(8,128)}), f32[1024,6400]{0,1:T(8,128)}) %all-gather.2.cloned.1.call-update) | async-done | bytes 26214416 | tf_op jit(solution)/shard_map/all_gather | solution.py:41
  274.5 45.6 %fusion.8 = f32[1024,512]{0,1:T(8,128)S(1)} fusion(f32[1024,6400]{0,1:T(8,128)} %all-gather.2.cloned.1.call-done, f32[6400,512]{1,0:T(8,128)} %bitcast.27), kind=kOutput, calls=%fused_computation.40 | convolution fusion | flops 40265318400 | bytes 41418752 | tf_op jit(solution)/shard_map/dot_general | solution.py:40
  320.0 5.8 %gather_fusion.1 = f32[1536,1024]{1,0:T(8,128)} fusion(f32[1024,512]{0,1:T(8,128)S(1)} %fusion.8, s32[2048]{0:T(1024)S(1)} %pad_clamp_fusion), kind=kCustom, calls=%fused_computation.1 | custom fusion | bytes 12589056 | tf_op jit(solution)/shard_map/jit(_take)/gather | solution.py:50
  325.9 4.9 %select_select_fusion = f32[1024,16,96]{0,2,1:T(8,128)} fusion(f32[1024,16,96]{0,2,1:T(8,128)} %bitcast.23, pred[16,96]{1,0:T(8,128)(4,1)S(1)} %get-tuple-element.10, pred[16,96]{1,0:T(8,128)(4,1)S(1)} %get-tuple-element.9), kind=kLoop, calls=%fused_computation.4 | loop fusion | flops 3145728 | bytes 12585984 | tf_op jit(solution)/shard_map/jit(_where)/select_n | solution.py:51
  330.8 10.4 %all-to-all-start = ((f32[1024,16,96]{0,2,1:T(8,128)}), f32[1024,16,96]{0,2,1:T(8,128)}, u32[]{:S(2)}, u32[]{:S(2)}) async-start(f32[1024,16,96]{0,2,1:T(8,128)} %select_select_fusion), calls=%async_computation | async-start | bytes 12582912 | tf_op jit(solution)/shard_map/all_to_all | solution.py:52
  341.2 0.0 copy-start.1
  341.3 0.0 copy-done
  341.3 1.3 gather_fusion.2
  342.6 72.2 %all-to-all-done = f32[1024,16,96]{0,2,1:T(8,128)} async-done(((f32[1024,16,96]{0,2,1:T(8,128)}), f32[1024,16,96]{0,2,1:T(8,128)}, u32[]{:S(2)}, u32[]{:S(2)}) %all-to-all-start) | async-done | bytes 6291488 | tf_op jit(solution)/shard_map/all_to_all | solution.py:52
  414.8 3.4 reduce_sum.72
  418.2 0.0 copy-done.1
  418.2 0.9 divide_select_fusion
  (9 shorter events, 0.1 us)
Async XLA Ops:
  6.5 334.7 %copy-start = (f32[512]{0:T(512)S(1)}, f32[512]{0:T(512)}, u32[]{:S(2)}) copy-start(f32[512]{0:T(512)} %param.8) | copy-start | bytes 6148
  6.5 267.9 %all-gather.2.cloned.1.call-start = ((), (), s32[]{:S(2)}) async-start(), calls=%async_computation.1 | async-start | bytes 29491200 | tf_op jit(solution)/shard_map/all_gather | solution.py:41
  330.8 84.0 %all-to-all-start = ((f32[1024,16,96]{0,2,1:T(8,128)}), f32[1024,16,96]{0,2,1:T(8,128)}, u32[]{:S(2)}, u32[]{:S(2)}) async-start(f32[1024,16,96]{0,2,1:T(8,128)} %select_select_fusion), calls=%async_computation | async-start | bytes 12582912 | tf_op jit(solution)/shard_map/all_to_all | solution.py:52
  341.2 76.9 %copy-start.1 = (f32[1024]{0:T(1024)S(1)}, f32[1024]{0:T(1024)}, u32[]{:S(2)}) copy-start(f32[1024]{0:T(1024)} %param.9) | copy-start | bytes 12292
Sparse Core Ops, SparseCore 0:
  8.9 265.4 all-gather.1
